TPU v7x, 128 devices: a whole 4x4x4 slice. The times are simulated.
128 devices in a mesh: row: 8 (over x, z_lo), col: 16 (over z_hi, y, core).
Axes of the slice: x: 4, y: 4, z: 4 (z_hi: 2, z_lo: 2; z = z_hi * 2 + z_lo), core: 2. Of those that a mesh axis runs over, the one named last changes fastest.
Arguments:
- act_q: bfloat16 [1024, 8192], P('col', 'row'), may hold values from -6 to 6
- act_scale: float32 [1024, 64], P('col', 'row'), may hold values from 0.25 to 4
- grad_q: bfloat16 [1024, 8192], P('col', 'row'), may hold values from -6 to 6
- grad_scale: float32 [1024, 64], P('col', 'row'), may hold values from 0.25 to 4
- gate_pre: bfloat16 [1024, 28672], P('row', 'col'), may hold values from -6 to 6
- up_pre: bfloat16 [1024, 28672], P('row', 'col'), may hold values from -6 to 6
- gate_weight: bfloat16 [8192, 28672], P('row', 'col'), may hold values from -0.0625 to 0.0625
- up_weight: bfloat16 [8192, 28672], P('row', 'col'), may hold values from -0.0625 to 0.0625
- down_weight: bfloat16 [28672, 8192], P('col', 'row'), may hold values from -0.03125 to 0.03125
Outputs:
- act_grad: bfloat16 [1024, 8192], P('col', 'row')
- gate_grad: bfloat16 [8192, 28672], P('row', 'col')
- up_grad: bfloat16 [8192, 28672], P('row', 'col')
- down_grad: bfloat16 [28672, 8192], P('col', 'row')
All inputs are finite; a program needn't handle non-finite values.
Results may differ from a plain program's by a relative error of at most 0.027.
Values may be sent and summed in bfloat16 or wider, within the bound.
A program may use at most 128 MiB of HBM per device.

v0:
```python
import math

import jax
import jax.numpy as jnp
from jax import lax
from jax.sharding import PartitionSpec as P


def dequant(values, scales):
    tok, width = values.shape
    blocks = values.astype(jnp.float32).reshape(tok, width // 128, 128) * scales[:, :, None]
    return blocks.reshape(tok, width).astype(jnp.bfloat16)


def contract_last(left, right):
    return lax.dot_general(
        left, right, (((1,), (1,)), ((), ())), preferred_element_type=jnp.float32
    )


def contract_first(left, right):
    return lax.dot_general(
        left, right, (((0,), (0,)), ((), ())), preferred_element_type=jnp.float32
    )


def pointwise(hidden_grad, gate_pre, up_pre):
    gate_val = gate_pre.astype(jnp.float32)
    up_val = up_pre.astype(jnp.float32)
    sigmoid_gate = jax.nn.sigmoid(gate_val)
    hidden = (gate_val * sigmoid_gate * up_val).astype(jnp.bfloat16)
    gate_delta = (
        hidden_grad * up_val * sigmoid_gate * (1.0 + gate_val * (1.0 - sigmoid_gate))
    ).astype(jnp.bfloat16)
    up_delta = (hidden_grad * gate_val * sigmoid_gate).astype(jnp.bfloat16)
    return (hidden, gate_delta, up_delta)


def shards(
    act_q, act_scale, grad_q, grad_scale, gate_pre, up_pre, gate_weight, up_weight, down_weight
):
    inputs = dequant(act_q, act_scale)
    out_grad = dequant(grad_q, grad_scale)
    inputs_all, out_grad_all = (
        lax.all_gather(inputs, "col", axis=0, tiled=True),
        lax.all_gather(out_grad, "col", axis=0, tiled=True),
    )
    total_tokens = gate_pre.shape[0] * lax.axis_size("row")
    factor = 1.0 / math.sqrt(total_tokens)
    hidden_grad = lax.psum_scatter(
        contract_last(out_grad_all, down_weight).astype(jnp.bfloat16),
        "row",
        scatter_dimension=0,
        tiled=True,
    ).astype(jnp.float32)
    hidden, gate_delta, up_delta = pointwise(hidden_grad, gate_pre, up_pre)
    hidden_all, gate_all, up_all = (
        lax.all_gather(hidden, "row", axis=0, tiled=True),
        lax.all_gather(gate_delta, "row", axis=0, tiled=True),
        lax.all_gather(up_delta, "row", axis=0, tiled=True),
    )
    down_grad = (contract_first(hidden_all, out_grad_all) * factor).astype(jnp.bfloat16)
    gate_grad = (contract_first(inputs_all, gate_all) * factor).astype(jnp.bfloat16)
    up_grad = (contract_first(inputs_all, up_all) * factor).astype(jnp.bfloat16)
    act_grad = lax.psum_scatter(
        (contract_last(gate_all, gate_weight) + contract_last(up_all, up_weight)).astype(
            jnp.bfloat16
        ),
        "col",
        scatter_dimension=0,
        tiled=True,
    )
    return (act_grad, gate_grad, up_grad, down_grad)


def solution(mesh):
    in_specs = (
        P("col", "row"),
        P("col", "row"),
        P("col", "row"),
        P("col", "row"),
        P("row", "col"),
        P("row", "col"),
        P("row", "col"),
        P("row", "col"),
        P("col", "row"),
    )
    out_specs = (P("col", "row"), P("row", "col"), P("row", "col"), P("col", "row"))
    return jax.shard_map(shards, mesh=mesh, in_specs=in_specs, out_specs=out_specs, check_vma=False)
```

profile of v0, /device:TPU:30, one launch (start us, length us, event | category | flops | bytes accessed | tf_op | source)
XLA Modules:
  0.0 531.7 jit_solution(10239221527860680664)
XLA Ops:
  7.2 0.0 all-gather.6.cloned.1.call-start
  7.2 0.8 copy.13
  8.0 0.1 mul.58
  8.1 1.6 fusion.11
  9.7 0.0 all-gather.6.cloned.1.call-update
  9.8 0.0 reduce-scatter.3.cloned.1.call-start
  9.8 51.5 %all-gather.6.cloned.1.call-done = bf16[1024,1024]{1,0:T(8,128)(2,1)} async-done(((bf16[64,1024]{1,0:T(8,128)(2,1)}), bf16[1024,1024]{1,0:T(8,128)(2,1)}) %all-gather.6.cloned.1.call-update) | async-done | bytes 2097168 | tf_op jit(solution)/shard_map/all_gather | solution.py:46
  61.3 8.5 %convolution_convert_fusion = bf16[1024,1792]{1,0:T(8,128)(2,1)} fusion(bf16[1024,1024]{1,0:T(8,128)(2,1)} %all-gather.6.cloned.1.call-done, bf16[1792,1024]{1,0:T(8,128)(2,1)} %param.17), kind=kOutput, calls=%fused_computation.4 | convolution fusion | flops 3759931392 | bytes 9437184 | tf_op jit(solution)/shard_map/dot_general | solution.py:16
  69.8 0.0 copy-start
  69.8 0.0 copy-start.1
  69.8 0.0 copy-start.3
  69.8 0.0 copy-start.2
  69.8 0.0 reduce-scatter.3.cloned.1.call-update
  69.8 0.0 all-gather.8.cloned.1.call-start
  69.9 79.5 %reduce-scatter.3.cloned.1.call-done = bf16[128,1792]{1,0:T(8,128)(2,1)} async-done(((bf16[1024,1792]{1,0:T(8,128)(2,1)}), bf16[128,1792]{1,0:T(8,128)(2,1)}) %reduce-scatter.3.cloned.1.call-update) | async-done | bytes 458768 | tf_op jit(solution)/shard_map/reduce_scatter | solution.py:50
  149.3 0.0 copy-done
  149.3 0.0 copy-done.1
  149.3 2.6 fusion.3
  151.9 0.0 all-gather.8.cloned.1.call-update
  152.0 0.0 all-gather.10.cloned.1.call-start
  152.0 0.5 all-gather.10.cloned.1.call-update
  152.5 0.0 all-gather.12.cloned.1.call-start
  152.6 0.0 copy-done.3
  152.6 0.1 copy.14
  152.7 0.1 mul.67
  152.8 0.0 copy-done.2
  152.8 0.7 fusion.10
  153.5 0.0 all-gather.12.cloned.1.call-update
  153.5 0.0 all-gather.14.cloned.1.call-start
  153.6 0.5 all-gather.14.cloned.1.call-update
  154.1 0.2 reduce-scatter.5.cloned.1.call-start
  154.4 78.7 %all-gather.8.cloned.1.call-done = bf16[1024,1792]{1,0:T(8,128)(2,1)} async-done(((bf16[128,1792]{1,0:T(8,128)(2,1)}), bf16[1024,1792]{1,0:T(8,128)(2,1)}) %all-gather.8.cloned.1.call-update) | async-done | bytes 3670032 | tf_op jit(solution)/shard_map/all_gather | solution.py:59
  233.0 9.1 %fusion.12 = f32[1024,1024]{1,0:T(8,128)} fusion(bf16[1024,1792]{1,0:T(8,128)(2,1)} %all-gather.8.cloned.1.call-done, bf16[1024,1792]{1,0:T(8,128)(2,1)} %param.15), kind=kOutput, calls=%fused_computation.25 | convolution fusion | flops 3758096384 | bytes 11534336 | tf_op jit(solution)/shard_map/dot_general | solution.py:16
  242.1 74.1 %all-gather.10.cloned.1.call-done = bf16[1024,1792]{1,0:T(8,128)(2,1)} async-done(((bf16[128,1792]{1,0:T(8,128)(2,1)}), bf16[1024,1792]{1,0:T(8,128)(2,1)}) %all-gather.10.cloned.1.call-update) | async-done | bytes 3670032 | tf_op jit(solution)/shard_map/all_gather | solution.py:60
  316.2 9.7 %add_convert_fusion = bf16[1024,1024]{1,0:T(8,128)(2,1)} fusion(f32[1024,1024]{1,0:T(8,128)} %fusion.12, bf16[1024,1792]{1,0:T(8,128)(2,1)} %all-gather.10.cloned.1.call-done, bf16[1024,1792]{1,0:T(8,128)(2,1)} %param.16), kind=kOutput, calls=%fused_computation.3 | convolution fusion | flops 3760193536 | bytes 13631488 | tf_op jit(solution)/shard_map/dot_general | solution.py:16
  325.9 0.0 reduce-scatter.5.cloned.1.call-update
  325.9 41.9 %all-gather.12.cloned.1.call-done = bf16[1024,1024]{1,0:T(8,128)(2,1)} async-done(((bf16[64,1024]{1,0:T(8,128)(2,1)}), bf16[1024,1024]{1,0:T(8,128)(2,1)}) %all-gather.12.cloned.1.call-update) | async-done | bytes 2097168 | tf_op jit(solution)/shard_map/all_gather | solution.py:45
  367.8 0.0 copy-start.4
  367.8 0.0 copy-start.6
  367.8 8.7 %multiply_convert_fusion.1 = bf16[1024,1792]{1,0:T(8,128)(2,1)} fusion(bf16[1024,1024]{1,0:T(8,128)(2,1)} %all-gather.12.cloned.1.call-done, bf16[1024,1792]{1,0:T(8,128)(2,1)} %all-gather.10.cloned.1.call-done), kind=kOutput, calls=%fused_computation.1 | convolution fusion | flops 3761766400 | bytes 9437184 | tf_op jit(solution)/shard_map/dot_general | solution.py:22
  376.4 0.0 copy-done.4
  376.5 0.0 copy-done.6
  376.5 0.0 copy-start.5
  376.5 5.8 %multiply_convert_fusion.2 = bf16[1024,1792]{1,0:T(8,128)(2,1)} fusion(bf16[1024,1024]{1,0:T(8,128)(2,1)S(1)} %copy-done.6, bf16[1024,1792]{1,0:T(8,128)(2,1)S(1)} %copy-done.4), kind=kOutput, calls=%fused_computation.2 | convolution fusion | flops 3761766400 | bytes 9437184 | tf_op jit(solution)/shard_map/dot_general | solution.py:22
  382.2 66.5 %all-gather.14.cloned.1.call-done = bf16[1024,1792]{1,0:T(8,128)(2,1)} async-done(((bf16[128,1792]{1,0:T(8,128)(2,1)}), bf16[1024,1792]{1,0:T(8,128)(2,1)}) %all-gather.14.cloned.1.call-update) | async-done | bytes 3670032 | tf_op jit(solution)/shard_map/all_gather | solution.py:58
  448.7 0.0 copy-done.5
  448.7 7.5 %multiply_convert_fusion = bf16[1792,1024]{1,0:T(8,128)(2,1)} fusion(bf16[1024,1792]{1,0:T(8,128)(2,1)} %all-gather.14.cloned.1.call-done, bf16[1024,1024]{1,0:T(8,128)(2,1)S(1)} %copy-done.5), kind=kOutput, calls=%fused_computation | convolution fusion | flops 3761766400 | bytes 9437184 | tf_op jit(solution)/shard_map/dot_general | solution.py:22
  456.2 68.7 %reduce-scatter.5.cloned.1.call-done = bf16[64,1024]{1,0:T(8,128)(2,1)} async-done(((bf16[1024,1024]{1,0:T(8,128)(2,1)}), bf16[64,1024]{1,0:T(8,128)(2,1)}) %reduce-scatter.5.cloned.1.call-update) | async-done | bytes 131088 | tf_op jit(solution)/shard_map/reduce_scatter | solution.py:65
Async XLA Ops:
  7.2 54.1 %all-gather.6.cloned.1.call-start = ((), (), s32[]{:S(2)}) async-start(), calls=%async_computation.2 | async-start | bytes 2228224 | tf_op jit(solution)/shard_map/all_gather | solution.py:46
  9.8 139.6 %reduce-scatter.3.cloned.1.call-start = ((), (), s32[]{:S(2)}) async-start(), calls=%async_computation.3 | async-start | bytes 4128768 | tf_op jit(solution)/shard_map/reduce_scatter | solution.py:50
  69.8 79.6 %copy-start = (bf16[128,1792]{1,0:T(8,128)(2,1)S(1)}, bf16[128,1792]{1,0:T(8,128)(2,1)}, u32[]{:S(2)}) copy-start(bf16[128,1792]{1,0:T(8,128)(2,1)} %param.14) | copy-start | bytes 1376260
  69.8 79.6 %copy-start.1 = (bf16[128,1792]{1,0:T(8,128)(2,1)S(1)}, bf16[128,1792]{1,0:T(8,128)(2,1)}, u32[]{:S(2)}) copy-start(bf16[128,1792]{1,0:T(8,128)(2,1)} %param.13) | copy-start | bytes 1376260
  69.8 82.8 %copy-start.3 = (f32[64,8]{0,1:T(8,128)S(1)}, f32[64,8]{0,1:T(8,128)}, u32[]{:S(2)}) copy-start(f32[64,8]{0,1:T(8,128)} %param.10) | copy-start | bytes 6148
  69.8 83.0 %copy-start.2 = (bf16[64,1024]{1,0:T(8,128)(2,1)S(1)}, bf16[64,1024]{1,0:T(8,128)(2,1)}, u32[]{:S(2)}) copy-start(bf16[64,1024]{1,0:T(8,128)(2,1)} %param.9) | copy-start | bytes 393220
  69.8 163.2 %all-gather.8.cloned.1.call-start = ((), (), s32[]{:S(2)}) async-start(), calls=%async_computation.4 | async-start | bytes 4128768 | tf_op jit(solution)/shard_map/all_gather | solution.py:59
  152.0 164.2 %all-gather.10.cloned.1.call-start = ((), (), s32[]{:S(2)}) async-start(), calls=%async_computation.5 | async-start | bytes 4128768 | tf_op jit(solution)/shard_map/all_gather | solution.py:60
  152.5 215.2 %all-gather.12.cloned.1.call-start = ((), (), s32[]{:S(2)}) async-start(), calls=%async_computation.7 | async-start | bytes 2228224 | tf_op jit(solution)/shard_map/all_gather | solution.py:45
  153.5 295.2 %all-gather.14.cloned.1.call-start = ((), (), s32[]{:S(2)}) async-start(), calls=%async_computation.8 | async-start | bytes 4128768 | tf_op jit(solution)/shard_map/all_gather | solution.py:58
  154.1 370.8 %reduce-scatter.5.cloned.1.call-start = ((), (), s32[]{:S(2)}) async-start(), calls=%async_computation.6 | async-start | bytes 2228224 | tf_op jit(solution)/shard_map/reduce_scatter | solution.py:65
  367.8 8.7 %copy-start.4 = (bf16[1024,1792]{1,0:T(8,128)(2,1)S(1)}, bf16[1024,1792]{1,0:T(8,128)(2,1)}, u32[]{:S(2)}) copy-start(bf16[1024,1792]{1,0:T(8,128)(2,1)} %all-gather.8.cloned.1.call-done) | copy-start | bytes 11010052
  367.8 8.7 %copy-start.6 = (bf16[1024,1024]{1,0:T(8,128)(2,1)S(1)}, bf16[1024,1024]{1,0:T(8,128)(2,1)}, u32[]{:S(2)}) copy-start(bf16[1024,1024]{1,0:T(8,128)(2,1)} %all-gather.12.cloned.1.call-done) | copy-start | bytes 6291460
  376.5 72.3 %copy-start.5 = (bf16[1024,1024]{1,0:T(8,128)(2,1)S(1)}, bf16[1024,1024]{1,0:T(8,128)(2,1)}, u32[]{:S(2)}) copy-start(bf16[1024,1024]{1,0:T(8,128)(2,1)} %all-gather.6.cloned.1.call-done) | copy-start | bytes 6291460
Sparse Core Ops, SparseCore 0:
  11.0 50.2 all-gather.5
  69.9 79.3 reduce-scatter.2
  152.1 80.9 all-gather.7
  235.1 81.0 all-gather.9
  318.5 49.2 all-gather.11
  369.8 78.8 all-gather.13
  453.3 71.6 reduce-scatter.4
where the time goes:
time: 533 us; the launch traced here: 532 us
  waiting for transfers between devices  462 us (87%)
  matrix products  49.2 us (9%)
  between operations  14.2 us (3%)
    reduce_scatter x1, waiting for transfers between devices, shards(): lax.psum_scatter(contract_last(out_grad_all, down_weight).astype(jnp.bflo...  79.5 us
    all_gather x1, waiting for transfers between devices, shards(): lax.all_gather(gate_delta, 'row', axis=0, tiled=True)  78.7 us
    all_gather x1, waiting for transfers between devices, shards(): lax.all_gather(up_delta, 'row', axis=0, tiled=True)  74.1 us
    reduce_scatter x1, waiting for transfers between devices, shards(): lax.psum_scatter((contract_last(gate_all, gate_weight) + contract_last(up...  68.7 us
    all_gather x1, waiting for transfers between devices, shards(): lax.all_gather(hidden, 'row', axis=0, tiled=True)  66.5 us
    all_gather x1, waiting for transfers between devices, shards(): lax.all_gather(out_grad, 'col', axis=0, tiled=True)  51.5 us
    all_gather x1, waiting for transfers between devices, shards(): lax.all_gather(inputs, 'col', axis=0, tiled=True)  41.9 us
    dot_general x3, matrix products, contract_last(): lax.dot_general(left, right, (((1,), (1,)), ((), ())), preferred_element_...  27.3 us
  transfers between devices with their start and end apart: 7, of which 7 were waited for; matrix products, arithmetic and copies ran while one was open for 8% of the time, Pallas kernels for 0%

commit v1 on v0

v1 whole, which is shorter than its diff:
```python
import math

import jax
import jax.numpy as jnp
from jax import lax
from jax.experimental import pallas as pl
from jax.experimental.pallas import tpu as pltpu
from jax.sharding import PartitionSpec as P

MESH = pl.DeviceIdType.MESH
T, DB, FB = 1024, 1024, 1792
PR = 80
QR = 128 - PR
PA, QA = 48, 32
PB, QB = PR - PA, QR - QA
F32, BF16 = jnp.float32, jnp.bfloat16

N_SEMS = 3 * 16 + 15 + 2 * 17 + 21


def nt(a, b):
    return lax.dot_general(a, b, (((1,), (1,)), ((), ())), preferred_element_type=F32)


def rows(ref, start, n):
    return ref.at[pl.ds(pl.multiple_of(start, 16), n), :]


def kernel(
    act_q, act_scale, grad_q, grad_scale, gate_pre, up_pre, gate_w, up_w, down_w,
    act_grad, inputs_out, out_grad_out, hidden_out, gate_out, up_out,
    g_all, u_all, h_all, part, landed, og_all, in_all, dw, gw, uw,
    hid, gd, ud, act_part, sib_in, y_out, y_in, z_out, z_in, final,
    send_sems, recv_sems, local_sems,
):
    row, col = lax.axis_index("row"), lax.axis_index("col")
    x, z = lax.div(row, 2), lax.rem(row, 2)
    zh, y, core = lax.div(col, 8), lax.rem(lax.div(col, 2), 4), lax.rem(col, 2)
    xl, xr, xf = lax.rem(x + 3, 4), lax.rem(x + 1, 4), lax.rem(x + 2, 4)
    yl, yr, yf = lax.rem(y + 3, 4), lax.rem(y + 1, 4), lax.rem(y + 2, 4)
    oz, ozh, ocore = 1 - z, 1 - zh, 1 - core

    def rdev(xx, zz):
        return (xx * 2 + zz, col)

    def cidx(hh, yy, cc):
        return hh * 8 + yy * 2 + cc

    def cdev(hh, yy, cc):
        return (row, cidx(hh, yy, cc))

    zdev, ldev, rtdev = rdev(x, oz), rdev(xl, z), rdev(xr, z)
    hdev, yldev, yrdev, yfdev = cdev(ozh, y, core), cdev(zh, yl, core), cdev(zh, yr, core), cdev(zh, yf, core)
    sdev = cdev(zh, y, ocore)

    count = [0]
    pending = []

    def make(src, dst, dev):
        i = count[0]
        count[0] += 1
        return pltpu.make_async_remote_copy(
            src_ref=src, dst_ref=dst, send_sem=send_sems.at[i], recv_sem=recv_sems.at[i],
            device_id=dev, device_id_type=MESH,
        )

    def send(src, dst, dev):
        copy = make(src, dst, dev)
        copy.start()
        pending.append(copy)
        return copy

    local_count = [0]

    def local(src, dst):
        copy = pltpu.make_async_copy(src, dst, local_sems.at[local_count[0]])
        local_count[0] += 1
        copy.start()
        return copy

    g_load = local(gate_pre, rows(g_all, row * 128, 128))
    u_load = local(up_pre, rows(u_all, row * 128, 128))
    dw_load = local(down_w, dw)
    gw_load = local(gate_w, gw)
    uw_load = local(up_w, uw)

    for blk in range(8):
        lanes = pl.ds(blk * 128, 128)
        og_all[pl.ds(pl.multiple_of(col * 64, 64), 64), lanes] = (
            grad_q[:, lanes].astype(F32) * grad_scale[:, blk : blk + 1]
        ).astype(BF16)
        in_all[pl.ds(pl.multiple_of(col * 64, 64), 64), lanes] = (
            act_q[:, lanes].astype(F32) * act_scale[:, blk : blk + 1]
        ).astype(BF16)

    barrier = pltpu.get_barrier_semaphore()
    partners = (zdev, ldev, rtdev, hdev, yldev, yrdev, yfdev, sdev)
    for dev in partners:
        pl.semaphore_signal(barrier, inc=1, device_id=dev, device_id_type=MESH)
    pl.semaphore_wait(barrier, len(partners))

    def ctile(ref, hh, yy, cc, off=0, n=64):
        return rows(ref, cidx(hh, yy, cc) * 64 + off, n)

    def csend(ref, hh, yy, cc, dev, off=0, n=64):
        where = ctile(ref, hh, yy, cc, off, n)
        return send(where, where, dev)

    def col_own(ref):
        return dict(
            h=csend(ref, zh, y, core, hdev),
            r=csend(ref, zh, y, core, yrdev),
            l=csend(ref, zh, y, core, yldev),
            s=[csend(ref, zh, y, core, sdev)],
        )

    def col_mid(ref, c):
        c["h"].wait_recv()
        c["hr"] = csend(ref, ozh, y, core, yrdev)
        c["hl"] = csend(ref, ozh, y, core, yldev)
        c["s"].append(csend(ref, ozh, y, core, sdev))
        c["r"].wait_recv()
        c["fr"] = csend(ref, zh, yl, core, yrdev, 0, 32)
        c["s"].append(csend(ref, zh, yl, core, sdev))
        c["l"].wait_recv()
        c["fl"] = csend(ref, zh, yr, core, yldev, 32, 32)
        c["s"].append(csend(ref, zh, yr, core, sdev))

    def col_late(ref, c):
        c["hr"].wait_recv()
        c["hfr"] = csend(ref, ozh, yl, core, yrdev, 0, 32)
        c["s"].append(csend(ref, ozh, yl, core, sdev))
        c["hl"].wait_recv()
        c["hfl"] = csend(ref, ozh, yr, core, yldev, 32, 32)
        c["s"].append(csend(ref, ozh, yr, core, sdev))
        c["fr"].wait_recv()
        c["fl"].wait_recv()
        c["s"].append(csend(ref, zh, yf, core, sdev))
        c["hfr"].wait_recv()
        c["hfl"].wait_recv()
        c["s"].append(csend(ref, ozh, yf, core, sdev))

    def col_end(c):
        for copy in c["s"]:
            copy.wait_recv()

    def rsend(ref, xx, zz, off, n, dev):
        where = rows(ref, (xx * 2 + zz) * 128 + off, n)
        return send(where, where, dev)

    def row_own(ref):
        return dict(
            zp=rsend(ref, x, z, 0, PR, zdev),
            r=rsend(ref, x, z, 0, 128, rtdev),
            l=rsend(ref, x, z, 0, 128, ldev),
            zq=rsend(ref, x, z, PR, QR, zdev),
        )

    def row_mid(ref, c):
        c["zp"].wait_recv()
        c["pr"] = rsend(ref, x, oz, 0, PR, rtdev)
        c["pl"] = rsend(ref, x, oz, 0, PR, ldev)
        c["r"].wait_recv()
        c["fqr"] = rsend(ref, xl, z, PR + QA, QB, rtdev)
        c["zql"] = rsend(ref, xl, z, PR, QR, zdev)
        c["fpr"] = rsend(ref, xl, z, 0, PA, rtdev)
        c["l"].wait_recv()
        c["fql"] = rsend(ref, xr, z, PR, QA, ldev)
        c["zqr"] = rsend(ref, xr, z, PR, QR, zdev)
        c["fpl"] = rsend(ref, xr, z, PA, PB, ldev)

    def row_late(ref, c):
        c["pr"].wait_recv()
        c["gpr"] = rsend(ref, xl, oz, 0, PA, rtdev)
        c["pl"].wait_recv()
        c["gpl"] = rsend(ref, xr, oz, PA, PB, ldev)
        c["fqr"].wait_recv()
        c["zfr"] = rsend(ref, xf, z, PR + QA, QB, zdev)
        c["fql"].wait_recv()
        c["zfl"] = rsend(ref, xf, z, PR, QA, zdev)

    def row_end(c, names):
        for name in names:
            c[name].wait_recv()

    og = col_own(og_all)
    g_load.wait()
    gc = row_own(g_all)
    u_load.wait()
    uc = row_own(u_all)
    col_mid(og_all, og)
    col_late(og_all, og)
    inp = col_own(in_all)
    col_end(og)
    dw_load.wait()

    @pl.loop(0, FB // 256)
    def _(j):
        cols = pl.ds(pl.multiple_of(j * 256, 256), 256)
        part[:, cols] = nt(og_all[...], dw[cols, :]).astype(BF16)

    def prow(xx, zz, off):
        return (xx * 2 + zz) * 128 + off

    slot = [0]

    def psend(xx, zz, off, n, dev):
        at = slot[0]
        slot[0] += n
        return send(rows(part, prow(xx, zz, off), n), landed.at[pl.ds(at, n), :], dev), at

    def add(xx, zz, off, at, n):
        @pl.loop(0, n // 16)
        def _(i):
            here = pl.ds(pl.multiple_of(prow(xx, zz, off) + i * 16, 16), 16)
            there = pl.ds(pl.multiple_of(at + i * 16, 16), 16)
            part[here, :] = (part[here, :].astype(F32) + landed[there, :].astype(F32)).astype(BF16)

    order = (xf, xl, xr, x)
    zs = [psend(xx, oz, PR, QR, zdev) for xx in order]
    far_r = [psend(xf, zz, 0, PA, rtdev) for zz in (oz, z)]
    far_l = [psend(xf, zz, PA, PB, ldev) for zz in (oz, z)]
    row_mid(g_all, gc)
    for (copy, at), xx in zip(zs, order):
        copy.wait_recv()
        add(xx, z, PR, at, QR)
        if xx is xf:
            far_rq = psend(xf, z, PR + QA, QB, rtdev)
            far_lq = psend(xf, z, PR, QA, ldev)
    for (copy, at), zz in zip(far_r, (oz, z)):
        copy.wait_recv()
        add(xr, zz, 0, at, PA)
    nb_r = [psend(xr, oz, 0, PR, rtdev)]
    for (copy, at), zz in zip(far_l, (oz, z)):
        copy.wait_recv()
        add(xl, zz, PA, at, PB)
    nb_l = [psend(xl, oz, 0, PR, ldev)]
    far_rq[0].wait_recv()
    add(xr, z, PR + QA, far_rq[1], QB)
    nb_r.append(psend(xr, z, 0, 128, rtdev))
    far_lq[0].wait_recv()
    add(xl, z, PR, far_lq[1], QA)
    nb_l.append(psend(xl, z, 0, 128, ldev))

    row_mid(u_all, uc)
    row_late(g_all, gc)
    col_mid(in_all, inp)
    col_late(in_all, inp)

    nb_r[0][0].wait_recv()
    nb_l[0][0].wait_recv()
    add(x, oz, 0, nb_r[0][1], PR)
    add(x, oz, 0, nb_l[0][1], PR)
    last = psend(x, oz, 0, PR, zdev)
    row_late(u_all, uc)
    nb_r[1][0].wait_recv()
    nb_l[1][0].wait_recv()
    last[0].wait_recv()

    def own(lo, hi, landings):
        @pl.loop(lo // 16, hi // 16)
        def _(i):
            here = pl.ds(pl.multiple_of(row * 128 + i * 16, 16), 16)
            total = part[here, :].astype(F32)
            for at in landings:
                total = total + landed[pl.ds(pl.multiple_of(at + i * 16, 16), 16), :].astype(F32)
            h_all[here, :] = total.astype(BF16)

    own(0, PR, (nb_r[1][1], nb_l[1][1], last[1]))
    own(PR, 128, (nb_r[1][1], nb_l[1][1]))

    hc = row_own(h_all)

    col_end(inp)
    outs = [local(in_all, inputs_out), local(og_all, out_grad_out)]
    row_end(gc, ("zq", "zql", "zqr", "fpr", "fpl", "gpr", "gpl", "zfr", "zfl"))
    row_end(uc, ("zq", "zql", "zqr", "fpr", "fpl", "gpr", "gpl", "zfr", "zfl"))

    def pointwise(xx):
        @pl.loop(0, 16)
        def _(i):
            here = pl.ds(pl.multiple_of(xx * 256 + i * 16, 16), 16)
            for j in range(FB // 256):
                cols = pl.ds(j * 256, 256)
                gv = g_all[here, cols].astype(F32)
                uv = u_all[here, cols].astype(F32)
                hv = h_all[here, cols].astype(F32)
                s = jax.nn.sigmoid(gv)
                gs = gv * s
                hid[here, cols] = (gs * uv).astype(BF16)
                gd[here, cols] = (hv * uv * s * (1.0 + gv * (1.0 - s))).astype(BF16)
                ud[here, cols] = (hv * gs).astype(BF16)

    def group(k, xx):
        pointwise(xx)
        for ref, out in ((hid, hidden_out), (gd, gate_out), (ud, up_out)):
            outs.append(local(rows(ref, xx * 256, 256), rows(out, xx * 256, 256)))
        here = pl.ds(pl.multiple_of(xx * 256, 256), 256)

        @pl.loop(0, DB // 256)
        def _(j):
            cols = pl.ds(pl.multiple_of(j * 256, 256), 256)
            act_part[k, :, cols] = (nt(gd[here, :], gw[cols, :]) + nt(ud[here, :], uw[cols, :])).astype(BF16)

        return [
            send(act_part.at[k, pl.ds(pl.multiple_of(j * 128 + ocore * 64, 64), 64), :], sib_in.at[k, j], sdev)
            for j in range(2)
        ]

    def reduce_y(k, xx, sib):
        for j in range(2):
            sib[j].wait_recv()
            mine = act_part[k, pl.ds(pl.multiple_of(j * 128 + core * 64, 64), 64), :]
            y_out[k, j] = (mine.astype(F32) + sib_in[k, j].astype(F32)).astype(BF16)
        copies = []
        for step in (1, 2, 3):
            to = lax.rem(y + 4 - step, 4)
            copy = make(y_out.at[k, lax.rem(to, 2)], y_in.at[k, step - 1], cdev(zh, to, core))
            goes = lax.div(to, 2) == lax.rem(xx, 2)

            @pl.when(goes)
            def _():
                copy.start()

            copies.append((copy, goes))
        return copies

    def reduce_end(k, xx, copies, zcopy):
        @pl.when(lax.div(y, 2) == lax.rem(xx, 2))
        def _():
            for copy, _ in copies:
                copy.wait_recv()
            total = y_out[k, lax.rem(y, 2)].astype(F32)
            for i in range(3):
                total = total + y_in[k, i].astype(F32)

            @pl.when(lax.div(xx, 2) == zh)
            def _():
                final[...] = total

            @pl.when(lax.div(xx, 2) != zh)
            def _():
                z_out[...] = total.astype(BF16)
                zcopy.start()

        for copy, goes in copies:
            @pl.when(goes)
            def _():
                copy.wait_send()

    gw_load.wait()
    uw_load.wait()
    zcopy = make(z_out, z_in, hdev)

    row_mid(h_all, hc)
    hc["zq"].wait_recv()
    s0 = group(0, x)
    row_late(h_all, hc)
    y0 = reduce_y(0, x, s0)
    row_end(hc, ("zql",))
    s1 = group(1, xl)
    reduce_end(0, x, y0, zcopy)
    y1 = reduce_y(1, xl, s1)
    row_end(hc, ("zqr",))
    s2 = group(2, xr)
    reduce_end(1, xl, y1, zcopy)
    y2 = reduce_y(2, xr, s2)
    row_end(hc, ("fpr", "fpl", "gpr", "gpl", "zfr", "zfl"))
    s3 = group(3, xf)
    reduce_end(2, xr, y2, zcopy)
    y3 = reduce_y(3, xf, s3)
    reduce_end(3, xf, y3, zcopy)
    zcopy.wait()
    act_grad[...] = (final[...] + z_in[...].astype(F32)).astype(BF16)
    for copy in outs:
        copy.wait()
    for copy in pending:
        copy.wait_send()
    assert count[0] == N_SEMS, count[0]


def exchange(*args):
    any_spec = pl.BlockSpec(memory_space=pl.ANY)
    vmem = pl.BlockSpec(memory_space=pltpu.VMEM)
    shape = jax.ShapeDtypeStruct
    wide = pltpu.VMEM((T, FB), BF16)
    return pl.pallas_call(
        kernel,
        out_shape=(
            shape((64, DB), BF16),
            shape((T, DB), BF16),
            shape((T, DB), BF16),
            shape((T, FB), BF16),
            shape((T, FB), BF16),
            shape((T, FB), BF16),
        ),
        in_specs=[vmem] * 4 + [any_spec] * 5,
        out_specs=(vmem,) + (any_spec,) * 5,
        scratch_shapes=[
            wide, wide, wide, wide,
            pltpu.VMEM((4 * QR + 2 * PR + QR + 2 * (128 + PR) + PR, FB), BF16),
            pltpu.VMEM((T, DB), BF16),
            pltpu.VMEM((T, DB), BF16),
            pltpu.VMEM((FB, DB), BF16),
            pltpu.VMEM((DB, FB), BF16),
            pltpu.VMEM((DB, FB), BF16),
            wide, wide, wide,
            pltpu.VMEM((4, 256, DB), BF16),
            pltpu.VMEM((4, 2, 64, DB), BF16),
            pltpu.VMEM((4, 2, 64, DB), BF16),
            pltpu.VMEM((4, 3, 64, DB), BF16),
            pltpu.VMEM((64, DB), BF16),
            pltpu.VMEM((64, DB), BF16),
            pltpu.VMEM((64, DB), F32),
            pltpu.SemaphoreType.DMA((N_SEMS,)),
            pltpu.SemaphoreType.DMA((N_SEMS,)),
            pltpu.SemaphoreType.DMA((32,)),
        ],
        compiler_params=pltpu.CompilerParams(
            collective_id=0, has_side_effects=True, vmem_limit_bytes=60 * 2**20
        ),
        name="exchange",
    )(*args)


def contract_first(left, right):
    return lax.dot_general(left, right, (((0,), (0,)), ((), ())), preferred_element_type=F32)


def shards(*args):
    act_grad, inputs, out_grad, hidden, gate, up = exchange(*args)
    factor = 1.0 / math.sqrt(T)
    down_grad = (contract_first(hidden, out_grad) * factor).astype(BF16)
    gate_grad = (contract_first(inputs, gate) * factor).astype(BF16)
    up_grad = (contract_first(inputs, up) * factor).astype(BF16)
    return act_grad, gate_grad, up_grad, down_grad


def solution(mesh):
    rc, cr = P("row", "col"), P("col", "row")
    return jax.shard_map(
        shards,
        mesh=mesh,
        in_specs=(cr, cr, cr, cr, rc, rc, rc, rc, cr),
        out_specs=(cr, rc, rc, cr),
        check_vma=False,
    )
```

time: 533 us -> 163 us (0.31)
  waiting for transfers between devices: 462 us -> 0 us
  Pallas kernels: 0 us -> 138 us
  matrix products: 49.2 us -> 19.7 us
  between operations: 14.2 us -> 0.67 us
    all_gather x5 -> x0, waiting for transfers between devices: 313 us -> none  [the longest x1 78.7 us: shards(): lax.all_gather(gate_delta, 'row', axis=0, tiled=True)]
    reduce_scatter x2 -> x0, waiting for transfers between devices: 148 us -> none  [the longest x1 79.5 us: shards(): lax.psum_scatter(contract_last(out_grad_all, down_weight).astype(jnp.bflo...]
    pallas_call x0 -> x1, Pallas kernels: none -> 138 us  [exchange(): pl.pallas_call(kernel, out_shape=(shape((64, DB), BF16), shape((T, DB), B...]
    dot_general x3 -> x0, matrix products: 27.3 us -> none  [contract_last(): lax.dot_general(left, right, (((1,), (1,)), ((), ())), preferred_element_...]
  transfers between devices with their start and end apart: 7 -> 0, of which waited for: 7 -> 0; matrix products, arithmetic and copies ran while one was open for 8% -> 0% of each run, Pallas kernels for 0% -> 0%
where the time goes in v1:
time: 163 us; the launch traced here: 162 us
  Pallas kernels  138 us (85%)
  matrix products  19.7 us (12%)
  local copies, waits for them, and re-layouts  3.44 us (2%)
    pallas_call x1, Pallas kernels, exchange(): pl.pallas_call(kernel, out_shape=(shape((64, DB), BF16), shape((T, DB), B...  138 us
    dot_general x3, matrix products, contract_first(): lax.dot_general(left, right, (((0,), (0,)), ((), ())), preferred_element_...  19.7 us
    unnamed x13, local copies, waits for them, and re-layouts  3.44 us

profile of v1, /device:TPU:30, one launch (start us, length us, event | category | flops | bytes accessed | tf_op | source)
XLA Modules:
  0.0 161.5 jit_solution(11495072488751458478)
XLA Ops:
  0.6 1.4 copy.13.act_scale
  2.0 1.4 copy.14.grad_scale
  3.4 137.7 %exchange.1 = (bf16[64,1024]{1,0:T(8,128)(2,1)}, bf16[1024,1024]{1,0:T(8,128)(2,1)}, bf16[1024,1024]{1,0:T(8,128)(2,1)}, bf16[1024,1792]{1,0:T(8,128)(2,1)}, bf1...) custom-call(bf16[64,1024]{1,0:T(8,128)(2,1)} %act_q.1, f32[64,8]{1,0:T(8,128)} %copy.13.act_scale, ...), custom_call_target="tpu_custom_call" | custom-call | tf_op jit(solution)/shard_map/exchange/pallas_call | solution.py:387
  141.1 0.0 copy-start.2
  141.1 0.0 copy-start.4
  141.1 8.7 %multiply_convert_fusion.2 = bf16[1024,1792]{1,0:T(8,128)(2,1)} fusion(bf16[1024,1024]{1,0:T(8,128)(2,1)} %get-tuple-element.11, bf16[1024,1792]{1,0:T(8,128)(2,1)} %get-tuple-element.12), kind=kOutput, calls=%fused_computation.2 | convolution fusion | flops 3761766400 | bytes 9437184 | tf_op jit(solution)/shard_map/dot_general | solution.py:427
  149.8 0.0 copy-done.2
  149.8 0.0 copy-done.4
  149.8 0.0 copy-start.1
  149.8 0.0 copy-start.3
  149.8 5.5 %multiply_convert_fusion.1 = bf16[1024,1792]{1,0:T(8,128)(2,1)} fusion(bf16[1024,1024]{1,0:T(8,128)(2,1)S(1)} %copy-done.4, bf16[1024,1792]{1,0:T(8,128)(2,1)S(1)} %copy-done.2), kind=kOutput, calls=%fused_computation.1 | convolution fusion | flops 3761766400 | bytes 9437184 | tf_op jit(solution)/shard_map/dot_general | solution.py:427
  155.4 0.0 copy-done.1
  155.4 0.0 copy-done.3
  155.4 0.0 copy-start
  155.4 5.5 %multiply_convert_fusion = bf16[1792,1024]{1,0:T(8,128)(2,1)} fusion(bf16[1024,1792]{1,0:T(8,128)(2,1)S(1)} %copy-done.1, bf16[1024,1024]{1,0:T(8,128)(2,1)S(1)} %copy-done.3), kind=kOutput, calls=%fused_computation | convolution fusion | flops 3761766400 | bytes 9437184 | tf_op jit(solution)/shard_map/dot_general | solution.py:427
  160.9 0.0 copy-done
  160.9 0.7 copy.16
Async XLA Ops:
  141.1 8.7 %copy-start.2 = (bf16[1024,1792]{1,0:T(8,128)(2,1)S(1)}, bf16[1024,1792]{1,0:T(8,128)(2,1)}, u32[]{:S(2)}) copy-start(bf16[1024,1792]{1,0:T(8,128)(2,1)} %get-tuple-element.13) | copy-start | bytes 11010052
  141.1 8.7 %copy-start.4 = (bf16[1024,1024]{1,0:T(8,128)(2,1)S(1)}, bf16[1024,1024]{1,0:T(8,128)(2,1)}, u32[]{:S(2)}) copy-start(bf16[1024,1024]{1,0:T(8,128)(2,1)} %get-tuple-element.11) | copy-start | bytes 6291460
  149.8 5.5 %copy-start.1 = (bf16[1024,1792]{1,0:T(8,128)(2,1)S(1)}, bf16[1024,1792]{1,0:T(8,128)(2,1)}, u32[]{:S(2)}) copy-start(bf16[1024,1792]{1,0:T(8,128)(2,1)} %get-tuple-element.14) | copy-start | bytes 11010052
  149.8 5.5 %copy-start.3 = (bf16[1024,1024]{1,0:T(8,128)(2,1)S(1)}, bf16[1024,1024]{1,0:T(8,128)(2,1)}, u32[]{:S(2)}) copy-start(bf16[1024,1024]{1,0:T(8,128)(2,1)} %get-tuple-element.15) | copy-start | bytes 6291460
  155.4 5.5 %copy-start = (bf16[64,1024]{1,0:T(8,128)(2,1)S(1)}, bf16[64,1024]{1,0:T(8,128)(2,1)}, u32[]{:S(2)}) copy-start(bf16[64,1024]{1,0:T(8,128)(2,1)} %get-tuple-element.20) | copy-start | bytes 393220

commit v2 on v1

--- a/solution.py
+++ b/solution.py
@@ -9,28 +9,34 @@
 
 MESH = pl.DeviceIdType.MESH
 T, DB, FB = 1024, 1024, 1792
-PR = 80
-QR = 128 - PR
-PA, QA = 48, 32
+LIMIT = 46
+F32, BF16 = jnp.float32, jnp.bfloat16
+FACTOR = 1.0 / math.sqrt(T)
+SPLIT_G, SPLIT_H = (80, 48, 32, 16), (80, 48, 48, 32)
+SPLIT_U = (64, 64, 32, 32)
+PR, QR, PA, QA = 80, 48, 48, 32
 PB, QB = PR - PA, QR - QA
-F32, BF16 = jnp.float32, jnp.bfloat16
-
-N_SEMS = 3 * 16 + 15 + 2 * 17 + 21
+
+N_SEMS = 3 * 16 + 15 + 2 * 17 + 8 * 4 + 1
 
 
 def nt(a, b):
     return lax.dot_general(a, b, (((1,), (1,)), ((), ())), preferred_element_type=F32)
 
 
+def tn(a, b):
+    return lax.dot_general(a, b, (((0,), (0,)), ((), ())), preferred_element_type=F32)
+
+
 def rows(ref, start, n):
     return ref.at[pl.ds(pl.multiple_of(start, 16), n), :]
 
 
 def kernel(
     act_q, act_scale, grad_q, grad_scale, gate_pre, up_pre, gate_w, up_w, down_w,
-    act_grad, inputs_out, out_grad_out, hidden_out, gate_out, up_out,
-    g_all, u_all, h_all, part, landed, og_all, in_all, dw, gw, uw,
-    hid, gd, ud, act_part, sib_in, y_out, y_in, z_out, z_in, final,
+    act_grad, part, dw, in_t, ud,
+    g_all, u_all, h_all, landed, og_all, in_all, gw, uw,
+    hid, gd, act_part, sib_in, y_out, y_in, z_out, z_in, final,
     send_sems, recv_sems, local_sems,
 ):
     row, col = lax.axis_index("row"), lax.axis_index("col")
@@ -84,19 +90,21 @@
     gw_load = local(gate_w, gw)
     uw_load = local(up_w, uw)
 
-    for blk in range(8):
-        lanes = pl.ds(blk * 128, 128)
-        og_all[pl.ds(pl.multiple_of(col * 64, 64), 64), lanes] = (
-            grad_q[:, lanes].astype(F32) * grad_scale[:, blk : blk + 1]
-        ).astype(BF16)
-        in_all[pl.ds(pl.multiple_of(col * 64, 64), 64), lanes] = (
-            act_q[:, lanes].astype(F32) * act_scale[:, blk : blk + 1]
-        ).astype(BF16)
-
     barrier = pltpu.get_barrier_semaphore()
     partners = (zdev, ldev, rtdev, hdev, yldev, yrdev, yfdev, sdev)
     for dev in partners:
         pl.semaphore_signal(barrier, inc=1, device_id=dev, device_id_type=MESH)
+
+    act_s, grad_s = act_scale[...].T, grad_scale[...].T
+    for blk in range(8):
+        lanes = pl.ds(blk * 128, 128)
+        og_all[pl.ds(pl.multiple_of(col * 64, 64), 64), lanes] = (
+            grad_q[:, lanes].astype(F32) * grad_s[:, blk : blk + 1]
+        ).astype(BF16)
+        in_all[pl.ds(pl.multiple_of(col * 64, 64), 64), lanes] = (
+            act_q[:, lanes].astype(F32) * act_s[:, blk : blk + 1]
+        ).astype(BF16)
+
     pl.semaphore_wait(barrier, len(partners))
 
     def ctile(ref, hh, yy, cc, off=0, n=64):
@@ -148,7 +156,8 @@
         where = rows(ref, (xx * 2 + zz) * 128 + off, n)
         return send(where, where, dev)
 
-    def row_own(ref):
+    def row_own(ref, split):
+        PR, QR, _, _ = split
         return dict(
             zp=rsend(ref, x, z, 0, PR, zdev),
             r=rsend(ref, x, z, 0, 128, rtdev),
@@ -156,7 +165,9 @@
             zq=rsend(ref, x, z, PR, QR, zdev),
         )
 
-    def row_mid(ref, c):
+    def row_mid(ref, c, split):
+        PR, QR, PA, QA = split
+        PB, QB = PR - PA, QR - QA
         c["zp"].wait_recv()
         c["pr"] = rsend(ref, x, oz, 0, PR, rtdev)
         c["pl"] = rsend(ref, x, oz, 0, PR, ldev)
@@ -169,7 +180,9 @@
         c["zqr"] = rsend(ref, xr, z, PR, QR, zdev)
         c["fpl"] = rsend(ref, xr, z, PA, PB, ldev)
 
-    def row_late(ref, c):
+    def row_late(ref, c, split):
+        PR, QR, PA, QA = split
+        PB, QB = PR - PA, QR - QA
         c["pr"].wait_recv()
         c["gpr"] = rsend(ref, xl, oz, 0, PA, rtdev)
         c["pl"].wait_recv()
@@ -179,15 +192,20 @@
         c["fql"].wait_recv()
         c["zfl"] = rsend(ref, xf, z, PR, QA, zdev)
 
+    def sent(copies):
+        for copy in copies:
+            copy.wait_send()
+            pending[:] = [other for other in pending if other is not copy]
+
     def row_end(c, names):
         for name in names:
             c[name].wait_recv()
 
     og = col_own(og_all)
     g_load.wait()
-    gc = row_own(g_all)
+    gc = row_own(g_all, SPLIT_G)
     u_load.wait()
-    uc = row_own(u_all)
+    uc = row_own(u_all, SPLIT_U)
     col_mid(og_all, og)
     col_late(og_all, og)
     inp = col_own(in_all)
@@ -220,7 +238,7 @@
     zs = [psend(xx, oz, PR, QR, zdev) for xx in order]
     far_r = [psend(xf, zz, 0, PA, rtdev) for zz in (oz, z)]
     far_l = [psend(xf, zz, PA, PB, ldev) for zz in (oz, z)]
-    row_mid(g_all, gc)
+    row_mid(g_all, gc, SPLIT_G)
     for (copy, at), xx in zip(zs, order):
         copy.wait_recv()
         add(xx, z, PR, at, QR)
@@ -242,8 +260,8 @@
     add(xl, z, PR, far_lq[1], QA)
     nb_l.append(psend(xl, z, 0, 128, ldev))
 
-    row_mid(u_all, uc)
-    row_late(g_all, gc)
+    row_mid(u_all, uc, SPLIT_U)
+    row_late(g_all, gc, SPLIT_G)
     col_mid(in_all, inp)
     col_late(in_all, inp)
 
@@ -252,7 +270,7 @@
     add(x, oz, 0, nb_r[0][1], PR)
     add(x, oz, 0, nb_l[0][1], PR)
     last = psend(x, oz, 0, PR, zdev)
-    row_late(u_all, uc)
+    row_late(u_all, uc, SPLIT_U)
     nb_r[1][0].wait_recv()
     nb_l[1][0].wait_recv()
     last[0].wait_recv()
@@ -269,111 +287,138 @@
     own(0, PR, (nb_r[1][1], nb_l[1][1], last[1]))
     own(PR, 128, (nb_r[1][1], nb_l[1][1]))
 
-    hc = row_own(h_all)
+    hc = row_own(h_all, SPLIT_H)
 
     col_end(inp)
-    outs = [local(in_all, inputs_out), local(og_all, out_grad_out)]
     row_end(gc, ("zq", "zql", "zqr", "fpr", "fpl", "gpr", "gpl", "zfr", "zfl"))
     row_end(uc, ("zq", "zql", "zqr", "fpr", "fpl", "gpr", "gpl", "zfr", "zfl"))
 
-    def pointwise(xx):
-        @pl.loop(0, 16)
+    @pl.loop(0, T // 16)
+    def _(i):
+        here = pl.ds(pl.multiple_of(i * 16, 16), 16)
+        for j in range(FB // 256):
+            cols = pl.ds(j * 256, 256)
+            gv = g_all[here, cols].astype(F32)
+            hid[here, cols] = (gv * jax.nn.sigmoid(gv) * u_all[here, cols].astype(F32)).astype(BF16)
+
+    @pl.loop(0, FB // 256)
+    def _(j):
+        cols = pl.ds(pl.multiple_of(j * 256, 256), 256)
+        dw[cols, :] = (tn(hid[:, cols], og_all[...]) * FACTOR).astype(BF16)
+
+
+    places = [(xl, z), (xr, z), (x, z), (x, oz), (xl, oz), (xr, oz), (xf, z), (xf, oz)]
+    for pos, (xx, zz) in enumerate(places):
+        in_t[:, pos * 128 : pos * 128 + 128] = in_all[pl.ds(pl.multiple_of((xx * 2 + zz) * 128, 128), 128), :].T
+
+    def pointwise(at, to):
+        @pl.loop(0, 8)
         def _(i):
-            here = pl.ds(pl.multiple_of(xx * 256 + i * 16, 16), 16)
+            here = pl.ds(pl.multiple_of(at + i * 16, 16), 16)
+            there = pl.ds(pl.multiple_of(to + i * 16, 16), 16)
             for j in range(FB // 256):
                 cols = pl.ds(j * 256, 256)
                 gv = g_all[here, cols].astype(F32)
-                uv = u_all[here, cols].astype(F32)
                 hv = h_all[here, cols].astype(F32)
                 s = jax.nn.sigmoid(gv)
-                gs = gv * s
-                hid[here, cols] = (gs * uv).astype(BF16)
-                gd[here, cols] = (hv * uv * s * (1.0 + gv * (1.0 - s))).astype(BF16)
-                ud[here, cols] = (hv * gs).astype(BF16)
-
-    def group(k, xx):
-        pointwise(xx)
-        for ref, out in ((hid, hidden_out), (gd, gate_out), (ud, up_out)):
-            outs.append(local(rows(ref, xx * 256, 256), rows(out, xx * 256, 256)))
-        here = pl.ds(pl.multiple_of(xx * 256, 256), 256)
+                gd[there, cols] = (hv * u_all[here, cols].astype(F32) * s * (1.0 + gv * (1.0 - s))).astype(BF16)
+                ud[there, cols] = (hv * gv * s).astype(BF16)
+
+    def gate_half(half):
+        here = pl.ds(half * 512, 512)
+        part[here, :] = (jnp.dot(in_t[here, :], gd[...], preferred_element_type=F32) * FACTOR).astype(BF16)
+
+    def block(pos):
+        xx, zz = places[pos]
+        at = xx * 2 + zz
+        return pos, at, lax.rem(at, 4), lax.div(at, 4)
+
+    def group(blocks):
+        here = pl.ds(blocks[0][0] * 128, 128 * len(blocks))
+        for pos, at, _, _ in blocks:
+            pointwise(at * 128, pos * 128)
 
         @pl.loop(0, DB // 256)
         def _(j):
             cols = pl.ds(pl.multiple_of(j * 256, 256), 256)
-            act_part[k, :, cols] = (nt(gd[here, :], gw[cols, :]) + nt(ud[here, :], uw[cols, :])).astype(BF16)
-
-        return [
-            send(act_part.at[k, pl.ds(pl.multiple_of(j * 128 + ocore * 64, 64), 64), :], sib_in.at[k, j], sdev)
-            for j in range(2)
-        ]
-
-    def reduce_y(k, xx, sib):
-        for j in range(2):
-            sib[j].wait_recv()
-            mine = act_part[k, pl.ds(pl.multiple_of(j * 128 + core * 64, 64), 64), :]
-            y_out[k, j] = (mine.astype(F32) + sib_in[k, j].astype(F32)).astype(BF16)
+            act_part[here, cols] = (nt(gd[here, :], gw[cols, :]) + nt(ud[here, :], uw[cols, :])).astype(BF16)
+
+        return [send(rows(act_part, pos * 128 + ocore * 64, 64), sib_in.at[pos], sdev) for pos, _, _, _ in blocks]
+
+    def reduce_y(blocks, sib):
         copies = []
-        for step in (1, 2, 3):
-            to = lax.rem(y + 4 - step, 4)
-            copy = make(y_out.at[k, lax.rem(to, 2)], y_in.at[k, step - 1], cdev(zh, to, core))
-            goes = lax.div(to, 2) == lax.rem(xx, 2)
-
-            @pl.when(goes)
+        for (i, _, yd, _), copy in zip(blocks, sib):
+            copy.wait_recv()
+            mine = act_part[pl.ds(pl.multiple_of(i * 128 + core * 64, 64), 64), :]
+            y_out[i] = (mine.astype(F32) + sib_in[i].astype(F32)).astype(BF16)
+            for step in (1, 2, 3):
+                copy = make(y_out.at[i], y_in.at[i, step - 1], cdev(zh, yd, core))
+                goes = lax.rem(yd + step, 4) == y
+
+                @pl.when(goes)
+                def _():
+                    copy.start()
+
+                copies.append((copy, goes))
+        return copies
+
+    def reduce_end(blocks, copies, zcopy):
+        for b, (i, _, yd, zd) in enumerate(blocks):
+            three = copies[3 * b : 3 * b + 3]
+
+            @pl.when(y == yd)
             def _():
-                copy.start()
-
-            copies.append((copy, goes))
-        return copies
-
-    def reduce_end(k, xx, copies, zcopy):
-        @pl.when(lax.div(y, 2) == lax.rem(xx, 2))
-        def _():
-            for copy, _ in copies:
-                copy.wait_recv()
-            total = y_out[k, lax.rem(y, 2)].astype(F32)
-            for i in range(3):
-                total = total + y_in[k, i].astype(F32)
-
-            @pl.when(lax.div(xx, 2) == zh)
-            def _():
-                final[...] = total
-
-            @pl.when(lax.div(xx, 2) != zh)
-            def _():
-                z_out[...] = total.astype(BF16)
-                zcopy.start()
-
-        for copy, goes in copies:
-            @pl.when(goes)
-            def _():
-                copy.wait_send()
+                for copy, _ in three:
+                    copy.wait_recv()
+                total = y_out[i].astype(F32)
+                for k in range(3):
+                    total = total + y_in[i, k].astype(F32)
+
+                @pl.when(zd == zh)
+                def _():
+                    final[...] = total
+
+                @pl.when(zd != zh)
+                def _():
+                    z_out[...] = total.astype(BF16)
+                    zcopy.start()
+
+            for copy, goes in three:
+                @pl.when(goes)
+                def _():
+                    copy.wait_send()
 
     gw_load.wait()
     uw_load.wait()
     zcopy = make(z_out, z_in, hdev)
 
-    row_mid(h_all, hc)
-    hc["zq"].wait_recv()
-    s0 = group(0, x)
-    row_late(h_all, hc)
-    y0 = reduce_y(0, x, s0)
-    row_end(hc, ("zql",))
-    s1 = group(1, xl)
-    reduce_end(0, x, y0, zcopy)
-    y1 = reduce_y(1, xl, s1)
-    row_end(hc, ("zqr",))
-    s2 = group(2, xr)
-    reduce_end(1, xl, y1, zcopy)
-    y2 = reduce_y(2, xr, s2)
-    row_end(hc, ("fpr", "fpl", "gpr", "gpl", "zfr", "zfl"))
-    s3 = group(3, xf)
-    reduce_end(2, xr, y2, zcopy)
-    y3 = reduce_y(3, xf, s3)
-    reduce_end(3, xf, y3, zcopy)
+    row_mid(h_all, hc, SPLIT_H)
+    work = [[block(0), block(1)], [block(2), block(3)], [block(4), block(5)], [block(6)], [block(7)]]
+    s0 = group(work[0])
+    row_end(hc, ("zq",))
+    s1 = group(work[1])
+    row_late(h_all, hc, SPLIT_H)
+    y0 = reduce_y(work[0], s0)
+    y1 = reduce_y(work[1], s1)
+    row_end(hc, ("zql", "zqr"))
+    s2 = group(work[2])
+    reduce_end(work[0], y0, zcopy)
+    reduce_end(work[1], y1, zcopy)
+    row_end(hc, ("fpr", "fpl"))
+    s3 = group(work[3])
+    y2 = reduce_y(work[2], s2)
+    row_end(hc, ("gpr", "gpl", "zfr", "zfl"))
+    s4 = group(work[4])
+    y3 = reduce_y(work[3], s3)
+    reduce_end(work[2], y2, zcopy)
+    sent([copy for copy, _ in zs + far_r + far_l + nb_r + nb_l + [far_rq, far_lq, last]])
+    y4 = reduce_y(work[4], s4)
+    gate_half(0)
+    reduce_end(work[3], y3, zcopy)
+    gate_half(1)
+    reduce_end(work[4], y4, zcopy)
     zcopy.wait()
     act_grad[...] = (final[...] + z_in[...].astype(F32)).astype(BF16)
-    for copy in outs:
-        copy.wait()
     for copy in pending:
         copy.wait_send()
     assert count[0] == N_SEMS, count[0]
@@ -382,33 +427,30 @@
 def exchange(*args):
     any_spec = pl.BlockSpec(memory_space=pl.ANY)
     vmem = pl.BlockSpec(memory_space=pltpu.VMEM)
-    shape = jax.ShapeDtypeStruct
     wide = pltpu.VMEM((T, FB), BF16)
     return pl.pallas_call(
         kernel,
         out_shape=(
-            shape((64, DB), BF16),
-            shape((T, DB), BF16),
-            shape((T, DB), BF16),
-            shape((T, FB), BF16),
-            shape((T, FB), BF16),
-            shape((T, FB), BF16),
+            pltpu.VMEM((64, DB), BF16),
+            pltpu.VMEM((DB, FB), BF16),
+            pltpu.VMEM((FB, DB), BF16),
+            pltpu.VMEM((DB, T), BF16),
+            pltpu.VMEM((T, FB), BF16),
         ),
         in_specs=[vmem] * 4 + [any_spec] * 5,
-        out_specs=(vmem,) + (any_spec,) * 5,
+        out_specs=(vmem,) * 5,
         scratch_shapes=[
-            wide, wide, wide, wide,
+            wide, wide, wide,
             pltpu.VMEM((4 * QR + 2 * PR + QR + 2 * (128 + PR) + PR, FB), BF16),
             pltpu.VMEM((T, DB), BF16),
             pltpu.VMEM((T, DB), BF16),
-            pltpu.VMEM((FB, DB), BF16),
             pltpu.VMEM((DB, FB), BF16),
             pltpu.VMEM((DB, FB), BF16),
-            wide, wide, wide,
-            pltpu.VMEM((4, 256, DB), BF16),
-            pltpu.VMEM((4, 2, 64, DB), BF16),
-            pltpu.VMEM((4, 2, 64, DB), BF16),
-            pltpu.VMEM((4, 3, 64, DB), BF16),
+            wide, wide,
+            pltpu.VMEM((T, DB), BF16),
+            pltpu.VMEM((8, 64, DB), BF16),
+            pltpu.VMEM((8, 64, DB), BF16),
+            pltpu.VMEM((8, 3, 64, DB), BF16),
             pltpu.VMEM((64, DB), BF16),
             pltpu.VMEM((64, DB), BF16),
             pltpu.VMEM((64, DB), F32),
@@ -417,23 +459,55 @@
             pltpu.SemaphoreType.DMA((32,)),
         ],
         compiler_params=pltpu.CompilerParams(
-            collective_id=0, has_side_effects=True, vmem_limit_bytes=60 * 2**20
+            collective_id=0, has_side_effects=True, vmem_limit_bytes=LIMIT * 2**20
         ),
         name="exchange",
     )(*args)
 
 
-def contract_first(left, right):
-    return lax.dot_general(left, right, (((0,), (0,)), ((), ())), preferred_element_type=F32)
-
-
-def shards(*args):
-    act_grad, inputs, out_grad, hidden, gate, up = exchange(*args)
-    factor = 1.0 / math.sqrt(T)
-    down_grad = (contract_first(hidden, out_grad) * factor).astype(BF16)
-    gate_grad = (contract_first(inputs, gate) * factor).astype(BF16)
-    up_grad = (contract_first(inputs, up) * factor).astype(BF16)
-    return act_grad, gate_grad, up_grad, down_grad
+STEPS = FB // 256
+
+
+def finish_kernel(in_t, delta, act, gate, down, up_grad, act_grad, gate_grad, down_grad, up, sems):
+    copies = [
+        pltpu.make_async_copy(act, act_grad, sems.at[0]),
+        pltpu.make_async_copy(down, down_grad, sems.at[1]),
+        pltpu.make_async_copy(gate, gate_grad, sems.at[2]),
+    ]
+    for copy in copies:
+        copy.start()
+    for half in range(2):
+        here = pl.ds(half * 512, 512)
+        up[here, :] = (jnp.dot(in_t[here, :], delta[...], preferred_element_type=F32) * FACTOR).astype(BF16)
+        copies.append(pltpu.make_async_copy(up.at[here, :], up_grad.at[here, :], sems.at[3 + half]))
+        copies[-1].start()
+    for copy in copies:
+        copy.wait()
+
+
+def finish(in_t, delta, act, gate, down):
+    any_spec = pl.BlockSpec(memory_space=pl.ANY)
+    vmem = pl.BlockSpec(memory_space=pltpu.VMEM)
+    up, act, gate, down = pl.pallas_call(
+        finish_kernel,
+        out_shape=(
+            jax.ShapeDtypeStruct((DB, FB), BF16),
+            jax.ShapeDtypeStruct(act.shape, BF16),
+            jax.ShapeDtypeStruct(gate.shape, BF16),
+            jax.ShapeDtypeStruct(down.shape, BF16),
+        ),
+        in_specs=[vmem] * 5,
+        out_specs=(any_spec,) * 4,
+        scratch_shapes=[pltpu.VMEM((DB, FB), BF16), pltpu.SemaphoreType.DMA((5,))],
+        compiler_params=pltpu.CompilerParams(vmem_limit_bytes=24 * 2**20),
+        name="finish",
+    )(in_t, delta, act, gate, down)
+    return act, gate, up, down
+
+
+def shards(act_q, act_scale, grad_q, grad_scale, *args):
+    act, gate, down, in_t, delta = exchange(act_q, act_scale.T, grad_q, grad_scale.T, *args)
+    return finish(in_t, delta, act, gate, down)
 
 
 def solution(mesh):

time: 163 us -> 144 us (0.88); the launches traced: 162 us -> 144 us
  matrix products: 19.7 us -> 0 us
  Pallas kernels: 138 us -> 144 us
  local copies, waits for them, and re-layouts: 3.44 us -> 0 us
    dot_general x3 -> x0, matrix products: 19.7 us -> none  [contract_first(): lax.dot_general(left, right, (((0,), (0,)), ((), ())), preferred_element_...]
    pallas_call x1 -> x2, Pallas kernels: 138 us -> 144 us  [the longest x1 138 us: exchange(): pl.pallas_call(kernel, out_shape=(pltpu.VMEM((64, DB), BF16), pltpu.VMEM(...]
    unnamed x13 -> x0, local copies, waits for them, and re-layouts: 3.44 us -> none
where the time goes in v2:
time: 144 us
  Pallas kernels  144 us (100%)
    pallas_call x1, Pallas kernels, exchange(): pl.pallas_call(kernel, out_shape=(pltpu.VMEM((64, DB), BF16), pltpu.VMEM(...  138 us
    pallas_call x1, Pallas kernels, finish(): pl.pallas_call(finish_kernel, out_shape=(jax.ShapeDtypeStruct((DB, FB), B...  5.24 us

profile of v2, /device:TPU:30, one launch (start us, length us, event | category | flops | bytes accessed | tf_op | source)
XLA Modules:
  0.0 144.3 jit_solution(7460302363976344763)
XLA Ops:
  0.6 138.3 %exchange.1 = (bf16[64,1024]{1,0:T(8,128)(2,1)S(1)}, bf16[1024,1792]{1,0:T(8,128)(2,1)S(1)}, bf16[1792,1024]{1,0:T(8,128)(2,1)S(1)}, bf16[1024,1024]{1,0:T(8,128)(2,1)S(1)}, bf16[1024,1792]{1,0:T(8,128)(2,1)S(1)}) custom-call(bf16[64,1024]{1,0:T(8,128)(2,1)} %act_q.1, f32[8,64]{1,0:T(8,128)} %bitcast.2, bf16[64,1024]{1,0:T(8,128)(2,1)} %grad_q.1, ...), custom_call_target="tpu_custom_call" | custom-call | tf_op jit(solution)/shard_map/exchange/pallas_call | solution.py:431
  138.9 5.2 %finish.1 = (bf16[1024,1792]{1,0:T(8,128)(2,1)}, bf16[64,1024]{1,0:T(8,128)(2,1)}, bf16[1024,1792]{1,0:T(8,128)(2,1)}, bf16[1792,1024]{1,0:T(8,128)(2,1)}) custom-call(bf16[1024,1024]{1,0:T(8,128)(2,1)S(1)} %get-tuple-element.13.in_t, bf16[1024,1792]{1,0:T(8,128)(2,1)S(1)} %get-tuple-element.14.delta, bf16[64,1024]{1,0:T(8,128)(2,1)S(1)} %get-tuple-element.15.act, ...), custom_call_target="tpu_custom_call" | custom-call | tf_op jit(solution)/shard_map/finish/pallas_call | solution.py:491

commit v3 on v2

--- a/solution.py
+++ b/solution.py
@@ -17,7 +17,7 @@
 PR, QR, PA, QA = 80, 48, 48, 32
 PB, QB = PR - PA, QR - QA
 
-N_SEMS = 3 * 16 + 15 + 2 * 17 + 8 * 4 + 1
+N_SEMS = 3 * 16 + 15 + 2 * 17 + 8 * 7 + 1
 
 
 def nt(a, b):
@@ -34,9 +34,9 @@
 
 def kernel(
     act_q, act_scale, grad_q, grad_scale, gate_pre, up_pre, gate_w, up_w, down_w,
-    act_grad, part, dw, in_t, ud,
-    g_all, u_all, h_all, landed, og_all, in_all, gw, uw,
-    hid, gd, act_part, sib_in, y_out, y_in, z_out, z_in, final,
+    act_grad, part, dw, g_all,
+    u_all, h_all, landed, og_all, in_all, gw, uw,
+    hid, gd, ud, in_t, act_part, sib_in, y_out, y_far, y_in, z_out, z_in, final,
     send_sems, recv_sems, local_sems,
 ):
     row, col = lax.axis_index("row"), lax.axis_index("col")
@@ -56,7 +56,7 @@
         return (row, cidx(hh, yy, cc))
 
     zdev, ldev, rtdev = rdev(x, oz), rdev(xl, z), rdev(xr, z)
-    hdev, yldev, yrdev, yfdev = cdev(ozh, y, core), cdev(zh, yl, core), cdev(zh, yr, core), cdev(zh, yf, core)
+    hdev, yldev, yrdev = cdev(ozh, y, core), cdev(zh, yl, core), cdev(zh, yr, core)
     sdev = cdev(zh, y, ocore)
 
     count = [0]
@@ -91,7 +91,7 @@
     uw_load = local(up_w, uw)
 
     barrier = pltpu.get_barrier_semaphore()
-    partners = (zdev, ldev, rtdev, hdev, yldev, yrdev, yfdev, sdev)
+    partners = (zdev, ldev, rtdev, hdev, yldev, yrdev, sdev)
     for dev in partners:
         pl.semaphore_signal(barrier, inc=1, device_id=dev, device_id_type=MESH)
 
@@ -324,9 +324,9 @@
                 gd[there, cols] = (hv * u_all[here, cols].astype(F32) * s * (1.0 + gv * (1.0 - s))).astype(BF16)
                 ud[there, cols] = (hv * gv * s).astype(BF16)
 
-    def gate_half(half):
-        here = pl.ds(half * 512, 512)
-        part[here, :] = (jnp.dot(in_t[here, :], gd[...], preferred_element_type=F32) * FACTOR).astype(BF16)
+    def weight_grad(delta, total, quarter):
+        here = pl.ds(quarter * 256, 256)
+        total[here, :] = (jnp.dot(in_t[here, :], delta[...], preferred_element_type=F32) * FACTOR).astype(BF16)
 
     def block(pos):
         xx, zz = places[pos]
@@ -345,34 +345,65 @@
 
         return [send(rows(act_part, pos * 128 + ocore * 64, 64), sib_in.at[pos], sdev) for pos, _, _, _ in blocks]
 
+    LO, HI = pl.ds(0, 32), pl.ds(32, 32)
+
     def reduce_y(blocks, sib):
-        copies = []
+        result = []
         for (i, _, yd, _), copy in zip(blocks, sib):
             copy.wait_recv()
             mine = act_part[pl.ds(pl.multiple_of(i * 128 + core * 64, 64), 64), :]
             y_out[i] = (mine.astype(F32) + sib_in[i].astype(F32)).astype(BF16)
-            for step in (1, 2, 3):
-                copy = make(y_out.at[i], y_in.at[i, step - 1], cdev(zh, yd, core))
-                goes = lax.rem(yd + step, 4) == y
-
-                @pl.when(goes)
+            where = lax.rem(y + 4 - yd, 4)
+
+            def half(src, dst, dev):
+                return make(y_out.at[i, src, :], dst.at[src, :], dev)
+
+            c = dict(
+                where=where,
+                far_lo=half(LO, y_far.at[i], yldev),
+                far_hi=half(HI, y_far.at[i], yrdev),
+                l_hi=half(HI, y_in.at[i, 0], yldev),
+                l_lo=half(LO, y_in.at[i, 0], yldev),
+                r_lo=half(LO, y_in.at[i, 1], yrdev),
+                r_hi=half(HI, y_in.at[i, 1], yrdev),
+            )
+
+            @pl.when(where == 2)
+            def _():
+                c["far_lo"].start()
+                c["far_hi"].start()
+
+            @pl.when(where == 1)
+            def _():
+                c["l_hi"].start()
+
+            @pl.when(where == 3)
+            def _():
+                c["r_lo"].start()
+
+            result.append(c)
+        return result
+
+    def relay(blocks, copies):
+        for (i, _, _, _), c in zip(blocks, copies):
+            for at, part_of, far, on in ((1, LO, "far_lo", "l_lo"), (3, HI, "far_hi", "r_hi")):
+
+                @pl.when(c["where"] == at)
                 def _():
-                    copy.start()
-
-                copies.append((copy, goes))
-        return copies
+                    c[far].wait_recv()
+                    y_out[i, part_of, :] = (
+                        y_out[i, part_of, :].astype(F32) + y_far[i, part_of, :].astype(F32)
+                    ).astype(BF16)
+                    c[on].start()
 
     def reduce_end(blocks, copies, zcopy):
-        for b, (i, _, yd, zd) in enumerate(blocks):
-            three = copies[3 * b : 3 * b + 3]
-
-            @pl.when(y == yd)
+        for (i, _, _, zd), c in zip(blocks, copies):
+
+            @pl.when(c["where"] == 0)
             def _():
-                for copy, _ in three:
-                    copy.wait_recv()
-                total = y_out[i].astype(F32)
-                for k in range(3):
-                    total = total + y_in[i, k].astype(F32)
+                for name in ("l_hi", "r_lo", "l_lo", "r_hi"):
+                    c[name].wait_recv()
+                total = y_out[i].astype(F32) + y_in[i, 0].astype(F32) + y_in[i, 1].astype(F32)
 
                 @pl.when(zd == zh)
                 def _():
@@ -383,10 +414,12 @@
                     z_out[...] = total.astype(BF16)
                     zcopy.start()
 
-            for copy, goes in three:
-                @pl.when(goes)
+            for at, names in ((2, ("far_lo", "far_hi")), (1, ("l_hi", "l_lo")), (3, ("r_lo", "r_hi"))):
+
+                @pl.when(c["where"] == at)
                 def _():
-                    copy.wait_send()
+                    for name in names:
+                        c[name].wait_send()
 
     gw_load.wait()
     uw_load.wait()
@@ -402,21 +435,31 @@
     y1 = reduce_y(work[1], s1)
     row_end(hc, ("zql", "zqr"))
     s2 = group(work[2])
-    reduce_end(work[0], y0, zcopy)
-    reduce_end(work[1], y1, zcopy)
+    relay(work[0], y0)
+    relay(work[1], y1)
     row_end(hc, ("fpr", "fpl"))
     s3 = group(work[3])
     y2 = reduce_y(work[2], s2)
+    reduce_end(work[0], y0, zcopy)
+    reduce_end(work[1], y1, zcopy)
     row_end(hc, ("gpr", "gpl", "zfr", "zfl"))
     s4 = group(work[4])
     y3 = reduce_y(work[3], s3)
-    reduce_end(work[2], y2, zcopy)
+    relay(work[2], y2)
     sent([copy for copy, _ in zs + far_r + far_l + nb_r + nb_l + [far_rq, far_lq, last]])
     y4 = reduce_y(work[4], s4)
-    gate_half(0)
+    weight_grad(gd, part, 0)
+    relay(work[3], y3)
+    weight_grad(gd, part, 1)
+    relay(work[4], y4)
+    reduce_end(work[2], y2, zcopy)
+    weight_grad(gd, part, 2)
     reduce_end(work[3], y3, zcopy)
-    gate_half(1)
+    weight_grad(gd, part, 3)
     reduce_end(work[4], y4, zcopy)
+    sent(list(gc.values()))
+    for quarter in range(4):
+        weight_grad(ud, g_all, quarter)
     zcopy.wait()
     act_grad[...] = (final[...] + z_in[...].astype(F32)).astype(BF16)
     for copy in pending:
@@ -434,23 +477,24 @@
             pltpu.VMEM((64, DB), BF16),
             pltpu.VMEM((DB, FB), BF16),
             pltpu.VMEM((FB, DB), BF16),
-            pltpu.VMEM((DB, T), BF16),
-            pltpu.VMEM((T, FB), BF16),
+            pltpu.VMEM((DB, FB), BF16),
         ),
         in_specs=[vmem] * 4 + [any_spec] * 5,
-        out_specs=(vmem,) * 5,
+        out_specs=(vmem,) * 4,
         scratch_shapes=[
-            wide, wide, wide,
+            wide, wide,
             pltpu.VMEM((4 * QR + 2 * PR + QR + 2 * (128 + PR) + PR, FB), BF16),
             pltpu.VMEM((T, DB), BF16),
             pltpu.VMEM((T, DB), BF16),
             pltpu.VMEM((DB, FB), BF16),
             pltpu.VMEM((DB, FB), BF16),
-            wide, wide,
+            wide, wide, wide,
+            pltpu.VMEM((DB, T), BF16),
             pltpu.VMEM((T, DB), BF16),
             pltpu.VMEM((8, 64, DB), BF16),
             pltpu.VMEM((8, 64, DB), BF16),
-            pltpu.VMEM((8, 3, 64, DB), BF16),
+            pltpu.VMEM((8, 64, DB), BF16),
+            pltpu.VMEM((8, 2, 64, DB), BF16),
             pltpu.VMEM((64, DB), BF16),
             pltpu.VMEM((64, DB), BF16),
             pltpu.VMEM((64, DB), F32),
@@ -465,49 +509,29 @@
     )(*args)
 
 
-STEPS = FB // 256
-
-
-def finish_kernel(in_t, delta, act, gate, down, up_grad, act_grad, gate_grad, down_grad, up, sems):
-    copies = [
-        pltpu.make_async_copy(act, act_grad, sems.at[0]),
-        pltpu.make_async_copy(down, down_grad, sems.at[1]),
-        pltpu.make_async_copy(gate, gate_grad, sems.at[2]),
-    ]
+def finish_kernel(*refs):
+    copies = [pltpu.make_async_copy(refs[i], refs[4 + i], refs[8].at[i]) for i in range(4)]
     for copy in copies:
         copy.start()
-    for half in range(2):
-        here = pl.ds(half * 512, 512)
-        up[here, :] = (jnp.dot(in_t[here, :], delta[...], preferred_element_type=F32) * FACTOR).astype(BF16)
-        copies.append(pltpu.make_async_copy(up.at[here, :], up_grad.at[here, :], sems.at[3 + half]))
-        copies[-1].start()
     for copy in copies:
         copy.wait()
 
 
-def finish(in_t, delta, act, gate, down):
-    any_spec = pl.BlockSpec(memory_space=pl.ANY)
-    vmem = pl.BlockSpec(memory_space=pltpu.VMEM)
-    up, act, gate, down = pl.pallas_call(
+def finish(*arrays):
+    return pl.pallas_call(
         finish_kernel,
-        out_shape=(
-            jax.ShapeDtypeStruct((DB, FB), BF16),
-            jax.ShapeDtypeStruct(act.shape, BF16),
-            jax.ShapeDtypeStruct(gate.shape, BF16),
-            jax.ShapeDtypeStruct(down.shape, BF16),
-        ),
-        in_specs=[vmem] * 5,
-        out_specs=(any_spec,) * 4,
-        scratch_shapes=[pltpu.VMEM((DB, FB), BF16), pltpu.SemaphoreType.DMA((5,))],
+        out_shape=tuple(jax.ShapeDtypeStruct(a.shape, BF16) for a in arrays),
+        in_specs=[pl.BlockSpec(memory_space=pltpu.VMEM)] * 4,
+        out_specs=(pl.BlockSpec(memory_space=pl.ANY),) * 4,
+        scratch_shapes=[pltpu.SemaphoreType.DMA((4,))],
         compiler_params=pltpu.CompilerParams(vmem_limit_bytes=24 * 2**20),
         name="finish",
-    )(in_t, delta, act, gate, down)
-    return act, gate, up, down
+    )(*arrays)
 
 
 def shards(act_q, act_scale, grad_q, grad_scale, *args):
-    act, gate, down, in_t, delta = exchange(act_q, act_scale.T, grad_q, grad_scale.T, *args)
-    return finish(in_t, delta, act, gate, down)
+    act, gate, down, up = exchange(act_q, act_scale.T, grad_q, grad_scale.T, *args)
+    return finish(act, gate, up, down)
 
 
 def solution(mesh):

time: 144 us -> 136 us (0.944); the launches traced: 144 us -> 135 us
  Pallas kernels: 144 us -> 134 us
    pallas_call x1, Pallas kernels: 138 us -> 130 us  [exchange(): pl.pallas_call(kernel, out_shape=(pltpu.VMEM((64, DB), BF16), pltpu.VMEM(...]
where the time goes in v3:
time: 136 us; the launch traced here: 135 us
  Pallas kernels  134 us (99%)
    pallas_call x1, Pallas kernels, exchange(): pl.pallas_call(kernel, out_shape=(pltpu.VMEM((64, DB), BF16), pltpu.VMEM(...  130 us
    pallas_call x1, Pallas kernels, finish(): pl.pallas_call(finish_kernel, out_shape=tuple((jax.ShapeDtypeStruct(a.sha...  4.33 us

profile of v3, /device:TPU:30, one launch (start us, length us, event | category | flops | bytes accessed | tf_op | source)
XLA Modules:
  0.0 134.9 jit_solution(17986619944482091475)
XLA Ops:
  0.6 129.7 %exchange.1 = (bf16[64,1024]{1,0:T(8,128)(2,1)S(1)}, bf16[1024,1792]{1,0:T(8,128)(2,1)S(1)}, bf16[1792,1024]{1,0:T(8,128)(2,1)S(1)}, bf16[1024,1792]{1,0:T(8,128)(2,1)S(1)}) custom-call(bf16[64,1024]{1,0:T(8,128)(2,1)} %act_q.1, f32[8,64]{1,0:T(8,128)} %bitcast.2, bf16[64,1024]{1,0:T(8,128)(2,1)} %grad_q.1, f32[8,64]{1,0:T(8,128)} %bitcast.3, ...), custom_call_target="tpu_custom_call" | custom-call | tf_op jit(solution)/shard_map/exchange/pallas_call | solution.py:474
  130.4 4.3 %finish.1 = (bf16[64,1024]{1,0:T(8,128)(2,1)}, bf16[1024,1792]{1,0:T(8,128)(2,1)}, bf16[1024,1792]{1,0:T(8,128)(2,1)}, bf16[1792,1024]{1,0:T(8,128)(2,1)}) custom-call(bf16[64,1024]{1,0:T(8,128)(2,1)S(1)} %get-tuple-element.8.refs_0_, bf16[1024,1792]{1,0:T(8,128)(2,1)S(1)} %get-tuple-element.9.refs_1_, bf16[1024,1792]{1,0:T(8,128)(2,1)S(1)} %get-tuple-element.10.refs_2_, ...), custom_call_target="tpu_custom_call" | custom-call | tf_op jit(solution)/shard_map/finish/pallas_call | solution.py:521

commit v4 on v3

--- a/solution.py
+++ b/solution.py
@@ -95,15 +95,15 @@
     for dev in partners:
         pl.semaphore_signal(barrier, inc=1, device_id=dev, device_id_type=MESH)
 
-    act_s, grad_s = act_scale[...].T, grad_scale[...].T
-    for blk in range(8):
-        lanes = pl.ds(blk * 128, 128)
-        og_all[pl.ds(pl.multiple_of(col * 64, 64), 64), lanes] = (
-            grad_q[:, lanes].astype(F32) * grad_s[:, blk : blk + 1]
-        ).astype(BF16)
-        in_all[pl.ds(pl.multiple_of(col * 64, 64), 64), lanes] = (
-            act_q[:, lanes].astype(F32) * act_s[:, blk : blk + 1]
-        ).astype(BF16)
+    def dequantize(values, scales, out):
+        by_token = scales[...].T
+        for blk in range(8):
+            lanes = pl.ds(blk * 128, 128)
+            out[pl.ds(pl.multiple_of(col * 64, 64), 64), lanes] = (
+                values[:, lanes].astype(F32) * by_token[:, blk : blk + 1]
+            ).astype(BF16)
+
+    dequantize(grad_q, grad_scale, og_all)
 
     pl.semaphore_wait(barrier, len(partners))
 
@@ -208,6 +208,7 @@
     uc = row_own(u_all, SPLIT_U)
     col_mid(og_all, og)
     col_late(og_all, og)
+    dequantize(act_q, act_scale, in_all)
     inp = col_own(in_all)
     col_end(og)
     dw_load.wait()

time: 136 us -> 136 us (level)
  no operation moved by 1% of the time
where the time goes in v4:
time: 136 us; the launch traced here: 135 us
  Pallas kernels  134 us (99%)
    pallas_call x1, Pallas kernels, exchange(): pl.pallas_call(kernel, out_shape=(pltpu.VMEM((64, DB), BF16), pltpu.VMEM(...  130 us
    pallas_call x1, Pallas kernels, finish(): pl.pallas_call(finish_kernel, out_shape=tuple((jax.ShapeDtypeStruct(a.sha...  4.33 us

profile of v4, /device:TPU:30, one launch (start us, length us, event | category | flops | bytes accessed | tf_op | source)
XLA Modules:
  0.0 134.8 jit_solution(10844040428423686345)
XLA Ops:
  0.6 129.6 %exchange.1 = (bf16[64,1024]{1,0:T(8,128)(2,1)S(1)}, bf16[1024,1792]{1,0:T(8,128)(2,1)S(1)}, bf16[1792,1024]{1,0:T(8,128)(2,1)S(1)}, bf16[1024,1792]{1,0:T(8,128)(2,1)S(1)}) custom-call(bf16[64,1024]{1,0:T(8,128)(2,1)} %act_q.1, f32[8,64]{1,0:T(8,128)} %bitcast.2, bf16[64,1024]{1,0:T(8,128)(2,1)} %grad_q.1, f32[8,64]{1,0:T(8,128)} %bitcast.3, ...), custom_call_target="tpu_custom_call" | custom-call | tf_op jit(solution)/shard_map/exchange/pallas_call | solution.py:475
  130.3 4.3 %finish.1 = (bf16[64,1024]{1,0:T(8,128)(2,1)}, bf16[1024,1792]{1,0:T(8,128)(2,1)}, bf16[1024,1792]{1,0:T(8,128)(2,1)}, bf16[1792,1024]{1,0:T(8,128)(2,1)}) custom-call(bf16[64,1024]{1,0:T(8,128)(2,1)S(1)} %get-tuple-element.8.refs_0_, bf16[1024,1792]{1,0:T(8,128)(2,1)S(1)} %get-tuple-element.9.refs_1_, bf16[1024,1792]{1,0:T(8,128)(2,1)S(1)} %get-tuple-element.10.refs_2_, ...), custom_call_target="tpu_custom_call" | custom-call | tf_op jit(solution)/shard_map/finish/pallas_call | solution.py:522
